TPU v7x, 32 devices: a whole 2x2x4 slice. The times are simulated.
32 devices in a mesh: rep: 2 (over y), ep: 16 (over z, x, core).
Axes of the slice: x: 2, y: 2, z: 4, core: 2. Of those that a mesh axis runs over, the one named last changes fastest.
Arguments:
- tokens: bfloat16 [256, 3072], P(('rep', 'ep')), parts along dimension 0, may hold values from -6 to 6
- expert_ids: int32 [256, 2], P(('rep', 'ep')), parts along dimension 0, may hold values from 0 to 7, all different within a row; in each aligned block of 8 rows (0 to 7, 8 to 15, ...) at most 4 rows name the same one
- gate_fixed: int32 [256, 2], P(('rep', 'ep')), parts along dimension 0, may hold values from 256 to 4096
- w_gate: bfloat16 [3072, 65536], P(None, 'ep'), may hold values from -0.109375 to 0.109375
- w_up: bfloat16 [3072, 65536], P(None, 'ep'), may hold values from -0.109375 to 0.109375
- w_down: bfloat16 [65536, 3072], P('ep'), may hold values from -0.0625 to 0.0625
Outputs:
- mixed: bfloat16 [256, 3072], P(('rep', 'ep')), parts along dimension 0
There are 2 independent parts, one for each index of `rep`. A program takes and returns all parts, laid end to end along the dimension named above; an argument that names none is the same for every part. Nothing has to cross between parts.
Inputs may be any that keep to these rules, and one draw needn't show every extreme that they name: `expert_ids`: each token names two different experts; among the 8 tokens of one device no expert is named more than 4 times, and in every draw some device names some expert exactly 4 times.
All inputs are finite; a program needn't handle non-finite values.
Results may differ from a plain program's by a relative error of at most 0.0057.
Values may be sent and summed in bfloat16 or wider, within the bound.
A program may use at most 128 MiB of HBM per device.

v0:
```python
import jax
import jax.numpy as jnp
from jax import lax
from jax.sharding import PartitionSpec as P

EXPERTS = 8
SLOT = 4


def expert_block(row_block, w_gate, w_up, w_down):
    gate_part = jnp.dot(row_block, w_gate, preferred_element_type=jnp.float32)
    up_part = jnp.dot(row_block, w_up, preferred_element_type=jnp.float32)
    hidden = (jax.nn.silu(gate_part) * up_part).astype(jnp.bfloat16)
    return jnp.dot(hidden, w_down, preferred_element_type=jnp.float32).astype(jnp.bfloat16)


def shards(tokens, expert_ids, gate_fixed, w_gate, w_up, w_down):
    devices_ep = lax.axis_size("ep")
    group_size = devices_ep // EXPERTS
    model_width = tokens.shape[1]
    expert_range = jnp.arange(EXPERTS, dtype=jnp.int32)
    slot_range = jnp.arange(SLOT, dtype=jnp.int32)
    chosen = jnp.any(expert_ids[:, :, None] == expert_range[None, None, :], axis=1)
    position = jnp.cumsum(chosen.astype(jnp.int32), axis=0) - 1
    gathered, gathered_ids = (
        lax.all_gather(tokens, "ep", axis=0, tiled=True),
        lax.all_gather(expert_ids.astype(jnp.bfloat16), "ep", axis=0, tiled=True),
    )
    my_expert = lax.axis_index("ep") // group_size
    every_ids = gathered_ids.astype(jnp.int32).reshape(devices_ep, -1, 2)
    routed = jnp.any(every_ids == my_expert, axis=2)
    routed_position = jnp.cumsum(routed.astype(jnp.int32), axis=1) - 1
    selector = (
        routed[:, None, :] & (routed_position[:, None, :] == slot_range[None, :, None])
    ).astype(jnp.bfloat16)
    slot_rows = jnp.einsum(
        "sjt,std->sjd",
        selector,
        gathered.reshape(devices_ep, -1, model_width),
        preferred_element_type=jnp.float32,
    ).astype(jnp.bfloat16)
    partial_value = expert_block(slot_rows.reshape(-1, model_width), w_gate, w_up, w_down)
    returned = lax.all_to_all(
        partial_value.reshape(devices_ep, SLOT, model_width),
        "ep",
        split_axis=0,
        concat_axis=0,
        tiled=True,
    )
    summed = jnp.sum(
        returned.astype(jnp.float32).reshape(EXPERTS, group_size, SLOT, model_width), axis=1
    )
    picked = summed[expert_range[None, :], jnp.clip(position, 0, SLOT - 1)]
    gate_values = gate_fixed.astype(jnp.float32) / 4096.0
    expert_weight = jnp.sum(
        jnp.where(
            expert_ids[:, :, None] == expert_range[None, None, :], gate_values[:, :, None], 0.0
        ),
        axis=1,
    )
    result = jnp.sum(jnp.where(chosen[:, :, None], expert_weight[:, :, None] * picked, 0.0), axis=1)
    return result.astype(jnp.bfloat16)


def solution(mesh):
    in_specs = (
        P(("rep", "ep"), None),
        P(("rep", "ep"), None),
        P(("rep", "ep"), None),
        P(None, "ep"),
        P(None, "ep"),
        P("ep", None),
    )
    out_specs = P(("rep", "ep"), None)
    return jax.shard_map(shards, mesh=mesh, in_specs=in_specs, out_specs=out_specs, check_vma=False)
```

profile of v0, /device:TPU:0, one launch (start us, length us, event | category | flops | bytes accessed | tf_op | source)
XLA Modules:
  0.0 94.1 jit_solution(13149973170688962772)
XLA Ops:
  0.0 0.7 convert_bitcast_fusion.1
  0.7 22.9 %all-gather = bf16[16,8,2]{1,2,0:T(2,128)(2,1)S(1)} all-gather(bf16[1,8,2]{1,2,0:T(2,128)(2,1)S(1)} %convert_bitcast_fusion.1), channel_id=1, replica_groups=mesh['rep'=2,'ep'=16] {'ep'}, dimensions={0}, use_global_device_ids=true | all-gather | bytes 544 | tf_op jit(solution)/shard_map/all_gather | solution.py:27
  23.7 0.2 reduce_window_sum.22
  23.8 19.8 %all_gather.7 = bf16[128,3072]{1,0:T(8,128)(2,1)S(1)} all-gather(bf16[8,3072]{1,0:T(8,128)(2,1)} %param.6), channel_id=1, replica_groups=mesh['rep'=2,'ep'=16] {'ep'}, dimensions={0}, use_global_device_ids=true | all-gather | bytes 835584 | tf_op jit(solution)/shard_map/all_gather | solution.py:26
  43.7 0.4 convolution_convert_fusion.1
  44.0 0.1 reshape.65
  44.1 10.5 %fusion.19 = f32[64,4096]{1,0:T(8,128)S(1)} fusion(bf16[64,3072]{1,0:T(8,128)(2,1)S(1)} %reshape.65, bf16[3072,4096]{1,0:T(8,128)(2,1)} %param.9), kind=kOutput, calls=%fused_computation.33 | convolution fusion | flops 1610612736 | bytes 26607616 | tf_op jit(solution)/shard_map/dot_general | solution.py:11
  54.6 0.0 copy-start
  54.6 0.0 copy-start.1
  54.6 19.9 %convolution_convert_fusion = bf16[64,3072]{1,0:T(8,128)(2,1)S(1)} fusion(bf16[4096,3072]{1,0:T(8,128)(2,1)} %param.11, bf16[64,3072]{1,0:T(8,128)(2,1)S(1)} %reshape.65, bf16[3072,4096]{1,0:T(8,128)(2,1)} %param.10, f32[64,4096]{1,0:T(8,128)S(1)} %fusion.19), kind=kOutput, calls=%fused_computation.3 | convolution fusion | flops 3222994944 | bytes 52166656 | tf_op jit(solution)/shard_map/dot_general | solution.py:14
  74.5 0.9 reshape.66
  75.4 3.6 %all-to-all-start = ((bf16[16,4,3072]{2,1,0:T(4,128)(2,1)}), bf16[16,4,3072]{2,1,0:T(4,128)(2,1)S(1)}, u32[]{:S(2)}, u32[]{:S(2)}) async-start(bf16[16,4,3072]{2,1,0:T(4,128)(2,1)} %reshape.66), calls=%async_computation | async-start | bytes 786432 | tf_op jit(solution)/shard_map/all_to_all | solution.py:43
  79.0 0.0 copy-done
  79.0 0.1 fusion.14
  79.1 0.1 reshape.72
  79.2 0.0 copy-done.1
  79.2 0.1 select_reduce_fusion
  79.3 11.9 %all-to-all-done = bf16[16,4,3072]{2,1,0:T(4,128)(2,1)S(1)} async-done(((bf16[16,4,3072]{2,1,0:T(4,128)(2,1)}), bf16[16,4,3072]{2,1,0:T(4,128)(2,1)S(1)}, u32[]{:S(2)}, u32[]{:S(2)}) %all-to-all-start) | async-done | bytes 393248 | tf_op jit(solution)/shard_map/all_to_all | solution.py:43
  91.1 0.2 convert_reduce_fusion
  91.4 1.8 %gather_fusion = f32[64,3072]{1,0:T(8,128)S(1)} fusion(f32[8,4,3072]{2,1,0:T(4,128)S(1)} %convert_reduce_fusion, s32[64]{0:T(128)S(1)} %reshape.72), kind=kCustom, calls=%fused_computation | custom fusion | bytes 1573376 | tf_op jit(solution)/shard_map/gather | solution.py:53
  93.2 0.9 fusion.7
  (7 shorter events, 0.1 us)
Async XLA Ops:
  54.6 24.4 %copy-start = (s32[8,2]{0,1:T(2,128)S(1)}, s32[8,2]{0,1:T(2,128)}, u32[]{:S(2)}) copy-start(s32[8,2]{0,1:T(2,128)} %param.7) | copy-start | bytes 196
  54.6 24.6 %copy-start.1 = (s32[8,2]{0,1:T(2,128)S(1)}, s32[8,2]{0,1:T(2,128)}, u32[]{:S(2)}) copy-start(s32[8,2]{0,1:T(2,128)} %param.8) | copy-start | bytes 196
  75.4 15.7 %all-to-all-start = ((bf16[16,4,3072]{2,1,0:T(4,128)(2,1)}), bf16[16,4,3072]{2,1,0:T(4,128)(2,1)S(1)}, u32[]{:S(2)}, u32[]{:S(2)}) async-start(bf16[16,4,3072]{2,1,0:T(4,128)(2,1)} %reshape.66), calls=%async_computation | async-start | bytes 786432 | tf_op jit(solution)/shard_map/all_to_all | solution.py:43
where the time goes:
time: 94.3 us; the launch traced here: 94.1 us
  blocking collectives  42.8 us (45%)
  matrix products  30.7 us (33%)
  waiting for transfers between devices  11.9 us (13%)
  starting transfers between devices  3.55 us (4%)
  local copies, waits for them, and re-layouts  2.88 us (3%)
  other arithmetic  2.26 us (2%)
    all_gather x1, blocking collectives, shards(): lax.all_gather(expert_ids.astype(jnp.bfloat16), 'ep', axis=0, tiled=True)  22.9 us
    dot_general x1, matrix products, expert_block(): jnp.dot(hidden, w_down, preferred_element_type=jnp.float32)  19.9 us
    all_gather x1, blocking collectives, shards(): lax.all_gather(tokens, 'ep', axis=0, tiled=True)  19.8 us
    all_to_all x1, waiting for transfers between devices, shards(): lax.all_to_all(partial_value.reshape(devices_ep, SLOT, model_width), 'ep'...  11.9 us
    dot_general x1, matrix products, expert_block(): gate_part = jnp.dot(row_block, w_gate, preferred_element_type=jnp.float32)  10.5 us
    all_to_all x1, starting transfers between devices, shards(): lax.all_to_all(partial_value.reshape(devices_ep, SLOT, model_width), 'ep'...  3.55 us
  transfers between devices with their start and end apart: 1, of which 1 were waited for; matrix products, arithmetic and copies ran while one was open for 0% of the time, Pallas kernels for 0%

commit v1 on v0

v1 whole, which is shorter than its diff:
```python
import functools

import jax
import jax.numpy as jnp
from jax import lax
from jax.experimental import pallas as pl
from jax.experimental.pallas import tpu as pltpu
from jax.sharding import PartitionSpec as P

EXPERTS = 8
SLOT = 4
QUARTERS = 4
PIECE = SLOT * QUARTERS
F_CHUNK = 256
N_CHUNK = 512
MAX_SLOTS = 8
MESH = pl.DeviceIdType.MESH
F32 = jnp.float32
BF16 = jnp.bfloat16


def iota(shape, dim):
    return lax.broadcasted_iota(jnp.int32, shape, dim)


def kernel(
    n_ep, f_chunk, n_chunk, slots,
    tok_ref, ids_ref, gate_ref, wg_ref, wu_ref, wd_ref, out_ref,
    wbuf, dbuf, send_buf, recv_buf, x_ref, hidden, pack, pair_recv, sum_buf, comb,
    w_sem, d_sem, a_send, a_recv, b_send, b_recv, c_send, c_recv, e_send, e_recv,
):
    n_chip = n_ep // 2
    chips_per_expert = n_chip // EXPERTS
    rep = lax.axis_index("rep")
    me = lax.axis_index("ep")
    core = lax.rem(me, 2)
    chip = me // 2
    partner = me + 1 - 2 * core
    width = tok_ref.shape[1]
    quarter = width // QUARTERS
    n_f = wg_ref.shape[1] // f_chunk
    n_n = width // n_chunk
    sub = n_chunk // QUARTERS
    n_tok = tok_ref.shape[0]
    rows = n_ep * SLOT

    def w_copies(f, slot):
        cols = pl.ds(pl.multiple_of(f * f_chunk, f_chunk), f_chunk)
        return (
            pltpu.make_async_copy(wg_ref.at[:, cols], wbuf.at[slot, 0], w_sem.at[slot, 0]),
            pltpu.make_async_copy(wu_ref.at[:, cols], wbuf.at[slot, 1], w_sem.at[slot, 1]),
        )

    def d_copy(n):
        cols = pl.ds(pl.multiple_of(n * n_chunk, n_chunk), n_chunk)
        return pltpu.make_async_copy(wd_ref.at[:, cols], dbuf.at[n], d_sem.at[n])

    barrier = pltpu.get_barrier_semaphore()

    def greet(i, _):
        to = lax.rem(chip + i, n_chip) * 2 + core
        pl.semaphore_signal(barrier, inc=1, device_id=(rep, to), device_id_type=MESH)
        return 0

    lax.fori_loop(1, n_chip, greet, 0)
    pl.semaphore_signal(barrier, inc=1, device_id=(rep, partner), device_id_type=MESH)

    def first(f, _):
        for copy in w_copies(f, f):
            copy.start()
        return 0

    lax.fori_loop(0, slots, first, 0)

    ids0 = ids_ref[:, 0:1]
    ids1 = ids_ref[:, 1:2]
    below = (iota((n_tok, n_tok), 1) < iota((n_tok, n_tok), 0)).astype(F32)

    def ranks(lanes, per_expert):
        lane = iota((n_tok, lanes), 1)
        expert = lane // (PIECE * per_expert)
        hit0, hit1 = ids0 == expert, ids1 == expert
        count = jnp.dot(below, (hit0 | hit1).astype(F32), preferred_element_type=F32)
        fits = count.astype(jnp.int32) == lax.rem(lane, SLOT)
        place = lax.rem(lane // SLOT, QUARTERS)
        return hit0 & fits, hit1 & fits, place

    hit0, hit1, place = ranks(EXPERTS * PIECE, 1)
    hit = hit0 | hit1
    piece = jnp.zeros((EXPERTS * PIECE, quarter), F32)
    for q in range(QUARTERS):
        mask = (hit & (place == q)).astype(F32).T.astype(BF16)
        piece += jnp.dot(
            mask, tok_ref[:, q * quarter:(q + 1) * quarter], preferred_element_type=F32
        )
    send_buf[...] = piece.astype(BF16)

    pl.semaphore_wait(barrier, n_chip)

    def rows_at(k):
        return pl.ds(pl.multiple_of(k * PIECE, PIECE), PIECE)

    def a_copy(to, source):
        return pltpu.make_async_remote_copy(
            src_ref=send_buf.at[rows_at(to // chips_per_expert)],
            dst_ref=recv_buf.at[rows_at(source * 2 + core)],
            send_sem=a_send.at[to],
            recv_sem=a_recv.at[source],
            device_id=(rep, to * 2 + core),
            device_id_type=MESH,
        )

    def b_copy(source, side):
        return pltpu.make_async_remote_copy(
            src_ref=recv_buf.at[rows_at(source * 2 + side)],
            dst_ref=recv_buf.at[rows_at(source * 2 + side)],
            send_sem=b_send.at[source],
            recv_sem=b_recv.at[source],
            device_id=(rep, partner),
            device_id_type=MESH,
        )

    def send_a(i, _):
        a_copy(lax.rem(chip + i, n_chip), chip).start()
        return 0

    lax.fori_loop(1, n_chip, send_a, 0)
    recv_buf[rows_at(me)] = send_buf[rows_at(chip // chips_per_expert)]
    b_copy(chip, core).start()

    def early(n, _):
        d_copy(n).start()
        return 0

    lax.fori_loop(0, n_n, early, 0)

    def forward(i, _):
        source = lax.rem(chip + n_chip - i, n_chip)
        a_copy(source, source).wait_recv()
        b_copy(source, core).start()
        return 0

    lax.fori_loop(1, n_chip, forward, 0)

    def arrived(i, _):
        b_copy(i, 1 - core).wait_recv()
        return 0

    lax.fori_loop(0, n_chip, arrived, 0)

    r = iota((rows, n_ep * PIECE), 0)
    l = iota((rows, n_ep * PIECE), 1)
    at = (r // SLOT) * PIECE + lax.rem(r, SLOT)
    for q in range(QUARTERS):
        take = (l == at + q * SLOT).astype(BF16)
        x_ref[:, q * quarter:(q + 1) * quarter] = jnp.dot(
            take, recv_buf[...], preferred_element_type=F32
        ).astype(BF16)

    def up_step(f, _):
        slot = lax.rem(f, slots)
        for copy in w_copies(f, slot):
            copy.wait()
        gate_part = jnp.dot(x_ref[...], wbuf[slot, 0], preferred_element_type=F32)
        up_part = jnp.dot(x_ref[...], wbuf[slot, 1], preferred_element_type=F32)
        value = gate_part / (1.0 + jnp.exp(-gate_part)) * up_part
        hidden[:, pl.ds(pl.multiple_of(f * f_chunk, f_chunk), f_chunk)] = value.astype(BF16)

        @pl.when(f + slots < n_f)
        def _():
            for copy in w_copies(f + slots, slot):
                copy.start()

        return 0

    lax.fori_loop(0, n_f, up_step, 0)

    half = n_chip * PIECE
    pr = iota((2 * half, rows), 0)
    side = lax.rem(pr // half + core, 2)
    owner = lax.rem(pr, half) // PIECE
    wanted = (owner * 2 + side) * SLOT + lax.rem(pr, SLOT)
    pack_hit = iota((2 * half, rows), 1) == wanted
    pack_place = lax.rem(pr // SLOT, QUARTERS)
    pack_q = [(pack_hit & (pack_place == q)).astype(BF16) for q in range(QUARTERS)]

    def c_copy(n):
        return pltpu.make_async_remote_copy(
            src_ref=pack.at[n, 1],
            dst_ref=pair_recv.at[n],
            send_sem=c_send.at[n],
            recv_sem=c_recv.at[n],
            device_id=(rep, partner),
            device_id_type=MESH,
        )

    def e_copy(n, to, source):
        return pltpu.make_async_remote_copy(
            src_ref=sum_buf.at[n, rows_at(to)],
            dst_ref=comb.at[n, rows_at(source)],
            send_sem=e_send.at[n, to],
            recv_sem=e_recv.at[n, source],
            device_id=(rep, to * 2 + core),
            device_id_type=MESH,
        )

    def down(n):
        d_copy(n).wait()
        part = jnp.dot(hidden[...], dbuf[n], preferred_element_type=F32).astype(BF16)
        packed = jnp.zeros((2 * half, sub), F32)
        for q in range(QUARTERS):
            packed += jnp.dot(
                pack_q[q], part[:, q * sub:(q + 1) * sub], preferred_element_type=F32
            )
        packed = packed.astype(BF16)
        pack[n, 0] = packed[:half]
        pack[n, 1] = packed[half:]
        c_copy(n).start()

    def reduce_send(n):
        c_copy(n).wait_recv()
        total = pack[n, 0].astype(F32) + pair_recv[n].astype(F32)
        sum_buf[n] = total.astype(BF16)

        def send_e(i, _):
            e_copy(n, lax.rem(chip + i, n_chip), chip).start()
            return 0

        lax.fori_loop(1, n_chip, send_e, 0)
        comb[n, rows_at(chip)] = sum_buf[n, rows_at(chip)]

    down(0)

    def down_step(n, _):
        down(n)
        reduce_send(n - 1)
        return 0

    lax.fori_loop(1, n_n, down_step, 0)
    reduce_send(n_n - 1)

    hit0, hit1, place = ranks(half, chips_per_expert)
    picks = jnp.concatenate(
        [(h & (place == q)).astype(F32) for h in (hit0, hit1) for q in range(QUARTERS)], axis=0
    ).astype(BF16)
    weights = gate_ref[...].astype(F32) / 4096.0
    g0, g1 = weights[:, 0:1], weights[:, 1:2]

    for n in range(n_n):

        def come(i, _):
            source = lax.rem(chip + n_chip - i, n_chip)
            e_copy(n, source, source).wait_recv()
            return 0

        lax.fori_loop(1, n_chip, come, 0)
        picked = jnp.dot(picks, comb[n], preferred_element_type=F32)
        for q in range(QUARTERS):
            k0 = picked[q * n_tok:(q + 1) * n_tok]
            k1 = picked[(QUARTERS + q) * n_tok:(QUARTERS + q + 1) * n_tok]
            start = n * n_chunk + q * sub
            out_ref[:, start:start + sub] = (g0 * k0 + g1 * k1).astype(BF16)

    def drain(i, _):
        to = lax.rem(chip + i, n_chip)
        a_copy(to, chip).wait_send()
        b_copy(to, core).wait_send()
        for n in range(n_n):
            e_copy(n, to, chip).wait_send()
        return 0

    lax.fori_loop(1, n_chip, drain, 0)
    b_copy(chip, core).wait_send()
    for n in range(n_n):
        c_copy(n).wait_send()


def shards(tokens, expert_ids, gate_fixed, w_gate, w_up, w_down):
    n_ep = lax.axis_size("ep")
    n_chip = n_ep // 2
    n_tok, width = tokens.shape
    ff = w_gate.shape[1]
    f_chunk = min(F_CHUNK, ff)
    n_chunk = min(N_CHUNK, width)
    n_f, n_n = ff // f_chunk, width // n_chunk
    slots = min(MAX_SLOTS, n_f)
    rows = n_ep * SLOT
    half = n_chip * PIECE
    sub = n_chunk // QUARTERS
    dma = pltpu.SemaphoreType.DMA
    vmem = pl.BlockSpec(memory_space=pltpu.VMEM)
    hbm = pl.BlockSpec(memory_space=pl.ANY)
    return pl.pallas_call(
        functools.partial(kernel, n_ep, f_chunk, n_chunk, slots),
        out_shape=jax.ShapeDtypeStruct((n_tok, width), BF16),
        in_specs=[vmem, vmem, vmem, hbm, hbm, hbm],
        out_specs=vmem,
        scratch_shapes=[
            pltpu.VMEM((slots, 2, width, f_chunk), BF16),
            pltpu.VMEM((n_n, ff, n_chunk), BF16),
            pltpu.VMEM((EXPERTS * PIECE, width // QUARTERS), BF16),
            pltpu.VMEM((n_ep * PIECE, width // QUARTERS), BF16),
            pltpu.VMEM((rows, width), BF16),
            pltpu.VMEM((rows, ff), BF16),
            pltpu.VMEM((n_n, 2, half, sub), BF16),
            pltpu.VMEM((n_n, half, sub), BF16),
            pltpu.VMEM((n_n, half, sub), BF16),
            pltpu.VMEM((n_n, half, sub), BF16),
            dma((slots, 2)),
            dma((n_n,)),
            dma((n_chip,)),
            dma((n_chip,)),
            dma((n_chip,)),
            dma((n_chip,)),
            dma((n_n,)),
            dma((n_n,)),
            dma((n_n, n_chip)),
            dma((n_n, n_chip)),
        ],
        compiler_params=pltpu.CompilerParams(
            collective_id=0, has_side_effects=True, vmem_limit_bytes=56 * 2**20
        ),
        cost_estimate=pl.CostEstimate(
            flops=6 * rows * width * ff, bytes_accessed=6 * width * ff, transcendentals=rows * ff
        ),
        name="moe",
    )(tokens, expert_ids, gate_fixed, w_gate, w_up, w_down)


def solution(mesh):
    in_specs = (
        P(("rep", "ep"), None),
        P(("rep", "ep"), None),
        P(("rep", "ep"), None),
        P(None, "ep"),
        P(None, "ep"),
        P("ep", None),
    )
    out_specs = P(("rep", "ep"), None)
    return jax.shard_map(shards, mesh=mesh, in_specs=in_specs, out_specs=out_specs, check_vma=False)
```

time: 94.3 us -> 47.1 us (0.50)
  blocking collectives: 42.8 us -> 0 us
  Pallas kernels: 0 us -> 42.7 us
  matrix products: 30.7 us -> 0 us
  waiting for transfers between devices: 11.9 us -> 0 us
  starting transfers between devices: 3.55 us -> 0 us
  other arithmetic: 2.26 us -> 0 us
  local copies, waits for them, and re-layouts: 2.88 us -> 4.11 us
    all_gather x2 -> x0, blocking collectives: 42.8 us -> none  [the longest x1 22.9 us: shards(): lax.all_gather(expert_ids.astype(jnp.bfloat16), 'ep', axis=0, tiled=True)]
    pallas_call x0 -> x1, Pallas kernels: none -> 42.7 us  [shards(): pl.pallas_call(functools.partial(kernel, n_ep, f_chunk, n_chunk, slots),...]
    dot_general x3 -> x0, matrix products: 30.7 us -> none  [the longest x1 19.9 us: expert_block(): jnp.dot(hidden, w_down, preferred_element_type=jnp.float32)]
    all_to_all x1 -> x0, waiting for transfers between devices: 11.9 us -> none  [shards(): lax.all_to_all(partial_value.reshape(devices_ep, SLOT, model_width), 'ep'...]
    unnamed x4 -> x3, local copies, waits for them, and re-layouts: 0.01 us -> 4.11 us
    all_to_all x1 -> x0, starting transfers between devices: 3.55 us -> none  [shards(): lax.all_to_all(partial_value.reshape(devices_ep, SLOT, model_width), 'ep'...]
    gather x1 -> x0, local copies, waits for them, and re-layouts: 1.81 us -> none  [shards(): picked = summed[expert_range[None, :], jnp.clip(position, 0, SLOT - 1)]]
    reduce_sum x3 -> x0, other arithmetic: 1.23 us -> none  [the longest x1 0.94 us: shards(): jnp.sum(jnp.where(chosen[:, :, None], expert_weight[:, :, None] * picked,...]
  transfers between devices with their start and end apart: 1 -> 0, of which waited for: 1 -> 0; matrix products, arithmetic and copies ran while one was open for 0% -> 0% of each run, Pallas kernels for 0% -> 0%
where the time goes in v1:
time: 47.1 us; the launch traced here: 46.9 us
  Pallas kernels  42.7 us (91%)
  local copies, waits for them, and re-layouts  4.11 us (9%)
    pallas_call x1, Pallas kernels, shards(): pl.pallas_call(functools.partial(kernel, n_ep, f_chunk, n_chunk, slots),...  42.7 us
    unnamed x3, local copies, waits for them, and re-layouts  4.11 us

profile of v1, /device:TPU:0, one launch (start us, length us, event | category | flops | bytes accessed | tf_op | source)
XLA Modules:
  0.0 46.9 jit_solution(14361109165229781428)
XLA Ops:
  0.0 1.3 %copy.7.ids_ref = s32[8,2]{1,0:T(8,128)} copy(s32[8,2]{0,1:T(2,128)} %param.7) | data formatting | bytes 128 | tf_op args[1]
  1.3 1.3 %copy.8.gate_ref = s32[8,2]{1,0:T(8,128)} copy(s32[8,2]{0,1:T(2,128)} %param.8) | data formatting | bytes 128 | tf_op args[2]
  2.7 42.7 %moe.1 = bf16[8,3072]{1,0:T(8,128)(2,1)} custom-call(bf16[8,3072]{1,0:T(8,128)(2,1)} %tok_ref.1, s32[8,2]{1,0:T(8,128)} %copy.7.ids_ref, s32[8,2]{1,0:T(8,128)} %copy.8.gate_ref, bf16[3072,4096]{1,0:T(8,128)(2,1)} %wg_ref.1, bf16[3072,4096]{1,0:T(8,128)(2,1)} %wu_ref.1, bf16[4096,3072]{1,0:T(8,128)(2,1)} %wd_ref.1), custom_call_target="tpu_custom_call" | custom-call | flops 4831838208 | bytes 75497472 | tf_op jit(solution)/shard_map/moe/pallas_call | solution.py:293
  45.4 1.4 %copy.10 = bf16[8,3072]{1,0:T(8,128)(2,1)} copy(bf16[8,3072]{1,0:T(8,128)(2,1)} %moe.1) | data formatting | bytes 98304

commit v2 on v1

--- a/solution.py
+++ b/solution.py
@@ -11,9 +11,10 @@
 SLOT = 4
 QUARTERS = 4
 PIECE = SLOT * QUARTERS
-F_CHUNK = 256
-N_CHUNK = 512
-MAX_SLOTS = 8
+F_CHUNK = 512
+N_CHUNK = 1024
+MAX_SLOTS = 4
+EARLY = 1
 MESH = pl.DeviceIdType.MESH
 F32 = jnp.float32
 BF16 = jnp.bfloat16
@@ -42,6 +43,7 @@
     n_n = width // n_chunk
     sub = n_chunk // QUARTERS
     n_tok = tok_ref.shape[0]
+    early = min(EARLY, n_n)
     rows = n_ep * SLOT
 
     def w_copies(f, slot):
@@ -72,8 +74,13 @@
 
     lax.fori_loop(0, slots, first, 0)
 
-    ids0 = ids_ref[:, 0:1]
-    ids1 = ids_ref[:, 1:2]
+    own = iota((n_tok, n_tok), 0) == iota((n_tok, n_tok), 1)
+
+    def column(row):
+        return jnp.sum(jnp.where(own, row.astype(F32), 0.0), axis=1, keepdims=True)
+
+    ids0 = column(ids_ref[0:1]).astype(jnp.int32)
+    ids1 = column(ids_ref[1:2]).astype(jnp.int32)
     below = (iota((n_tok, n_tok), 1) < iota((n_tok, n_tok), 0)).astype(F32)
 
     def ranks(lanes, per_expert):
@@ -128,11 +135,8 @@
     recv_buf[rows_at(me)] = send_buf[rows_at(chip // chips_per_expert)]
     b_copy(chip, core).start()
 
-    def early(n, _):
+    for n in range(early):
         d_copy(n).start()
-        return 0
-
-    lax.fori_loop(0, n_n, early, 0)
 
     def forward(i, _):
         source = lax.rem(chip + n_chip - i, n_chip)
@@ -170,6 +174,11 @@
         def _():
             for copy in w_copies(f + slots, slot):
                 copy.start()
+
+        @pl.when(f == max(n_f - slots - 1, 0))
+        def _():
+            for n in range(early, n_n):
+                d_copy(n).start()
 
         return 0
 
@@ -243,8 +252,7 @@
     picks = jnp.concatenate(
         [(h & (place == q)).astype(F32) for h in (hit0, hit1) for q in range(QUARTERS)], axis=0
     ).astype(BF16)
-    weights = gate_ref[...].astype(F32) / 4096.0
-    g0, g1 = weights[:, 0:1], weights[:, 1:2]
+    g0, g1 = column(gate_ref[0:1]) / 4096.0, column(gate_ref[1:2]) / 4096.0
 
     for n in range(n_n):
 
@@ -324,7 +332,7 @@
             flops=6 * rows * width * ff, bytes_accessed=6 * width * ff, transcendentals=rows * ff
         ),
         name="moe",
-    )(tokens, expert_ids, gate_fixed, w_gate, w_up, w_down)
+    )(tokens, expert_ids.T, gate_fixed.T, w_gate, w_up, w_down)
 
 
 def solution(mesh):

time: 47.1 us -> 41.8 us (0.89)
  local copies, waits for them, and re-layouts: 4.11 us -> 1.42 us
  Pallas kernels: 42.7 us -> 40.1 us
    unnamed x3 -> x1, local copies, waits for them, and re-layouts: 4.11 us -> 1.42 us
    pallas_call x1, Pallas kernels: 42.7 us -> 40.1 us  [shards(): pl.pallas_call(functools.partial(kernel, n_ep, f_chunk, n_chunk, slots),...]
where the time goes in v2:
time: 41.8 us; the launch traced here: 41.5 us
  Pallas kernels  40.1 us (96%)
  local copies, waits for them, and re-layouts  1.42 us (3%)
    pallas_call x1, Pallas kernels, shards(): pl.pallas_call(functools.partial(kernel, n_ep, f_chunk, n_chunk, slots),...  40.1 us
    unnamed x1, local copies, waits for them, and re-layouts  1.42 us

profile of v2, /device:TPU:0, one launch (start us, length us, event | category | flops | bytes accessed | tf_op | source)
XLA Modules:
  0.0 41.5 jit_solution(17922286598992400051)
XLA Ops:
  0.0 40.1 %moe.1 = bf16[8,3072]{1,0:T(8,128)(2,1)} custom-call(bf16[8,3072]{1,0:T(8,128)(2,1)} %tok_ref.1, s32[2,8]{1,0:T(2,128)} %bitcast.2, s32[2,8]{1,0:T(2,128)} %bitcast.3, bf16[3072,4096]{1,0:T(8,128)(2,1)} %wg_ref.1, bf16[3072,4096]{1,0:T(8,128)(2,1)} %wu_ref.1, bf16[4096,3072]{1,0:T(8,128)(2,1)} %wd_ref.1), custom_call_target="tpu_custom_call" | custom-call | flops 4831838208 | bytes 75497472 | tf_op jit(solution)/shard_map/moe/pallas_call | solution.py:301
  40.1 1.4 %copy.8 = bf16[8,3072]{1,0:T(8,128)(2,1)} copy(bf16[8,3072]{1,0:T(8,128)(2,1)} %moe.1) | data formatting | bytes 98304
